TPU v7x, 32 devices: a whole 2x2x4 slice. The times are simulated.
32 devices in a mesh: dp: 4 (over z), ctx: 8 (over y, x, core).
Axes of the slice: x: 2, y: 2, z: 4, core: 2. Of those that a mesh axis runs over, the one named last changes fastest.
Arguments:
- tokens: bfloat16 [8, 512, 2048], P('dp', 'ctx'), may hold values from -6 to 6
- block_order: int32 [8, 16], P('dp'), may hold values from 0 to 15, each once within a row
- ln_gain: bfloat16 [2048], P(('dp', 'ctx')), may hold values from 0.5 to 1.5
- ln_bias: bfloat16 [2048], P(('dp', 'ctx')), may hold values from -1.75 to 1.75
- w_qkv: bfloat16 [2048, 6144], P(('dp', 'ctx')), may hold values from -0.125 to 0.125
- b_qkv: bfloat16 [6144], P(('dp', 'ctx')), may hold values from -1.75 to 1.75
- w_dense: bfloat16 [2048, 2048], P(('dp', 'ctx')), may hold values from -1 to 1
- b_dense: bfloat16 [2048], P(('dp', 'ctx')), may hold values from -1.75 to 1.75
- w_fc1: bfloat16 [2048, 8192], P(('dp', 'ctx')), may hold values from -0.125 to 0.125
- b_fc1: bfloat16 [8192], P(('dp', 'ctx')), may hold values from -3 to 3
- w_fc2: bfloat16 [8192, 2048], P(('dp', 'ctx')), may hold values from -0.0625 to 0.0625
- b_fc2: bfloat16 [2048], P(('dp', 'ctx')), may hold values from -1.75 to 1.75
- cotangent: bfloat16 [8, 512, 2048], P('dp', 'ctx'), may hold values from -6 to 6
Outputs:
- output: bfloat16 [8, 512, 2048], P('dp', 'ctx')
- token_grad: bfloat16 [8, 512, 2048], P('dp', 'ctx')
- grad_ln_gain: float32 [2048], P(('dp', 'ctx'))
- grad_ln_bias: float32 [2048], P(('dp', 'ctx'))
- grad_w_qkv: float32 [2048, 6144], P(('dp', 'ctx'))
- grad_b_qkv: float32 [6144], P(('dp', 'ctx'))
- grad_w_dense: float32 [2048, 2048], P(('dp', 'ctx'))
- grad_b_dense: float32 [2048], P(('dp', 'ctx'))
- grad_w_fc1: float32 [2048, 8192], P(('dp', 'ctx'))
- grad_b_fc1: float32 [8192], P(('dp', 'ctx'))
- grad_w_fc2: float32 [8192, 2048], P(('dp', 'ctx'))
- grad_b_fc2: float32 [2048], P(('dp', 'ctx'))
Inputs may be any that keep to these rules, and one draw needn't show every extreme that they name: `block_order`: each row names every block of its sequence once.
All inputs are finite; a program needn't handle non-finite values.
Results may differ from a plain program's by a relative error of at most 0.014.
Values may be sent and summed in bfloat16 or wider, within the bound.
No kernel may reach another device: no remote copies, remote signals or barrier semaphores. Data moves between devices by JAX's collectives and lax.ppermute only.
A program may use at most 704 MiB of HBM per device.

v0:
```python
from functools import partial

import jax
import jax.numpy as jnp
from jax import lax
from jax.sharding import PartitionSpec as P

HEAD = 64
ROT = 32
ROPE_BASE = 10000


norm_eps = 1e-05


def passed_along(value, axis, steps):
    count = lax.axis_size(axis)
    pairs = [(source, (source + steps) % count) for source in range(count)]
    return lax.ppermute(value, axis, pairs)


def layer_norm(inputs, gain_vec, shift_vec):
    centre = inputs - jnp.mean(inputs, -1, keepdims=True)
    spread = jnp.mean(centre * centre, -1, keepdims=True)
    return centre * lax.rsqrt(spread + norm_eps) * gain_vec + shift_vec


def rotate(field, token_place, turn_sign):
    half_rot = ROT // 2
    freqs = jnp.asarray(ROPE_BASE, jnp.float32) ** (
        -(jnp.arange(half_rot, dtype=jnp.float32) * (2.0 / ROT))
    )
    angles = token_place.astype(jnp.float32)[..., None] * freqs
    cosine = jnp.cos(angles)[..., None, :]
    sine = turn_sign * jnp.sin(angles)[..., None, :]
    first = field[..., :half_rot]
    second = field[..., half_rot:ROT]
    return jnp.concatenate(
        [first * cosine - second * sine, second * cosine + first * sine, field[..., ROT:]], -1
    )


def block_places(order, device, block_len):
    slots = lax.dynamic_slice_in_dim(order, 2 * device, 2, 1)
    offsets = jnp.arange(block_len, dtype=jnp.int32)
    return (slots[:, :, None] * block_len + offsets[None, None, :]).reshape(
        order.shape[0], 2 * block_len
    )


def contract_last(left, right):
    return lax.dot_general(
        left, right, (((1,), (1,)), ((), ())), preferred_element_type=jnp.float32
    )


def contract_first(left, right):
    return lax.dot_general(
        left, right, (((0,), (0,)), ((), ())), preferred_element_type=jnp.float32
    )


def on_device(
    tokens,
    block_order,
    ln_gain,
    ln_bias,
    w_qkv,
    b_qkv,
    w_dense,
    b_dense,
    w_fc1,
    b_fc1,
    w_fc2,
    b_fc2,
    cotangent,
):
    micro_count, local_span, model_width = tokens.shape
    row_count = micro_count * local_span
    head_count = model_width // HEAD
    block_len = local_span // 2
    score_scale = HEAD ** (-0.5)
    ctx_count = lax.axis_size("ctx")
    ctx_index = lax.axis_index("ctx")
    down_rows = w_fc2.reshape(w_dense.shape[0], -1)
    vectors = (
        lax.all_gather(ln_gain, ("dp", "ctx"), axis=0, tiled=True),
        lax.all_gather(ln_bias, ("dp", "ctx"), axis=0, tiled=True),
        lax.all_gather(b_qkv, ("dp", "ctx"), axis=0, tiled=True),
        lax.all_gather(b_fc1, ("dp", "ctx"), axis=0, tiled=True),
        lax.all_gather(b_dense, ("dp", "ctx"), axis=0, tiled=True),
        lax.all_gather(b_fc2, ("dp", "ctx"), axis=0, tiled=True),
    )
    gain_full, shift_full, bias_qkv, bias_up, bias_dense, bias_down = [
        item.astype(jnp.float32) for item in vectors
    ]
    inputs = tokens.reshape(row_count, model_width).astype(jnp.float32)
    normed = layer_norm(inputs, gain_full, shift_full)
    normed_low = normed.astype(jnp.bfloat16)
    pieces = (
        lax.all_gather(w_qkv, ("dp", "ctx"), axis=0, tiled=True),
        lax.all_gather(w_fc1, ("dp", "ctx"), axis=0, tiled=True),
    )
    left = normed_low
    qkv_proj = jnp.dot(left, pieces[0], preferred_element_type=jnp.float32)
    up_proj = jnp.dot(left, pieces[1], preferred_element_type=jnp.float32)
    qkv_proj = qkv_proj + bias_qkv
    up_proj = up_proj + bias_up
    query_place = block_places(block_order, ctx_index, block_len)
    qkv_heads = qkv_proj.reshape(micro_count, local_span, 3, head_count, HEAD)
    query_low = rotate(qkv_heads[:, :, 0], query_place, 1.0).astype(jnp.bfloat16)
    key_low = rotate(qkv_heads[:, :, 1], query_place, 1.0).astype(jnp.bfloat16)
    value_low = qkv_heads[:, :, 2].astype(jnp.bfloat16)
    key_pair = jnp.stack(
        [
            key_low.reshape(micro_count, local_span, model_width),
            value_low.reshape(micro_count, local_span, model_width),
        ]
    )

    def block_scores(pair_now, source):
        key_place = block_places(block_order, source, block_len)
        key_blk = pair_now[0].reshape(micro_count, local_span, head_count, HEAD)
        value_blk = pair_now[1].reshape(micro_count, local_span, head_count, HEAD)
        scores = (
            jnp.einsum("mqhe,mkhe->mqhk", query_low, key_blk, preferred_element_type=jnp.float32)
            * score_scale
        )
        allowed = key_place[:, None, None, :] <= query_place[:, :, None, None]
        return (jnp.where(allowed, scores, -1e30), allowed, key_blk, value_blk)

    def attend(pair_now, source, state):
        running_max, running_sum, summed = state
        scores, allowed, key_blk, value_blk = block_scores(pair_now, source)
        new_max = jnp.maximum(running_max, jnp.max(scores, -1))
        weights = jnp.where(allowed, jnp.exp(scores - new_max[..., None]), 0.0)
        factor = jnp.exp(running_max - new_max)
        running_sum = running_sum * factor + jnp.sum(weights, -1)
        summed = summed * factor[..., None] + jnp.einsum(
            "mqhk,mkhe->mqhe",
            weights.astype(jnp.bfloat16),
            value_blk,
            preferred_element_type=jnp.float32,
        )
        return (new_max, running_sum, summed)

    first_state = (
        jnp.full((micro_count, local_span, head_count), -1e30, jnp.float32),
        jnp.zeros((micro_count, local_span, head_count), jnp.float32),
        jnp.zeros((micro_count, local_span, head_count, HEAD), jnp.float32),
    )
    first_state = attend(key_pair, ctx_index, first_state)

    def forward_turn(step_index, carry):
        pair_now, state = carry
        pair_now = passed_along(pair_now, "ctx", 1)
        source = (ctx_index - step_index + ctx_count) % ctx_count
        return (pair_now, attend(pair_now, source, state))

    _, (running_max, running_sum, summed) = lax.fori_loop(
        1, ctx_count, forward_turn, (key_pair, first_state)
    )
    attention = summed / running_sum[..., None]
    log_total = running_max + jnp.log(running_sum)
    attention_low = attention.reshape(row_count, model_width).astype(jnp.bfloat16)
    hidden_low = jax.nn.gelu(up_proj, approximate=True).astype(jnp.bfloat16)
    pieces = (
        lax.all_gather(w_dense, ("dp", "ctx"), axis=0, tiled=True),
        lax.all_gather(down_rows, ("dp", "ctx"), axis=0, tiled=True),
    )
    count = pieces[0].shape[0]
    ratio = pieces[1].shape[1] // model_width
    left = attention_low
    hidden_cols = hidden_low
    projected = jnp.dot(left, pieces[0], preferred_element_type=jnp.float32) + jnp.dot(
        hidden_cols,
        pieces[1].reshape(count * ratio, model_width),
        preferred_element_type=jnp.float32,
    )
    output = (
        (inputs + projected + bias_dense + bias_down)
        .astype(jnp.bfloat16)
        .reshape(micro_count, local_span, model_width)
    )
    grad_out = cotangent.reshape(row_count, model_width)
    grad_out_full = grad_out.astype(jnp.float32)
    pieces = (
        lax.all_gather(w_dense, ("dp", "ctx"), axis=0, tiled=True),
        lax.all_gather(down_rows, ("dp", "ctx"), axis=0, tiled=True),
    )
    count = pieces[0].shape[0]
    ratio = pieces[1].shape[1] // model_width
    grad_attn = contract_last(grad_out, pieces[0])
    grad_hid = contract_last(grad_out, pieces[1].reshape(count * ratio, model_width))
    grad_attention_low = grad_attn.astype(jnp.bfloat16).reshape(
        micro_count, local_span, head_count, HEAD
    )
    delta = jnp.sum(grad_attention_low.astype(jnp.float32) * attention, -1)

    def attend_back(pair_now, grads_pair, source, grad_query):
        scores, allowed, key_blk, value_blk = block_scores(pair_now, source)
        probability = jnp.where(allowed, jnp.exp(scores - log_total[..., None]), 0.0)
        grad_value = jnp.einsum(
            "mqhk,mqhe->mkhe",
            probability.astype(jnp.bfloat16),
            grad_attention_low,
            preferred_element_type=jnp.float32,
        )
        grad_prob = jnp.einsum(
            "mqhe,mkhe->mqhk", grad_attention_low, value_blk, preferred_element_type=jnp.float32
        )
        grad_scores = (probability * (grad_prob - delta[..., None])).astype(jnp.bfloat16)
        grad_query = grad_query + jnp.einsum(
            "mqhk,mkhe->mqhe", grad_scores, key_blk, preferred_element_type=jnp.float32
        )
        grad_key = jnp.einsum(
            "mqhk,mqhe->mkhe", grad_scores, query_low, preferred_element_type=jnp.float32
        )
        grads_pair = grads_pair + jnp.stack(
            [
                grad_key.reshape(micro_count, local_span, model_width),
                grad_value.reshape(micro_count, local_span, model_width),
            ]
        )
        return (grads_pair, grad_query)

    def pass_grads(grads_pair):
        return passed_along(grads_pair.astype(jnp.bfloat16), "ctx", 1).astype(grads_pair.dtype)

    grads_pair, grad_query = attend_back(
        key_pair,
        jnp.zeros((2, micro_count, local_span, model_width), jnp.float32),
        ctx_index,
        jnp.zeros((micro_count, local_span, head_count, HEAD), jnp.float32),
    )

    def backward_turn(step_index, carry):
        pair_now, grads_now, grad_q_now = carry
        pair_now = passed_along(pair_now, "ctx", 1)
        grads_now = pass_grads(grads_now)
        source = (ctx_index - step_index + ctx_count) % ctx_count
        grads_now, grad_q_now = attend_back(pair_now, grads_now, source, grad_q_now)
        return (pair_now, grads_now, grad_q_now)

    _, grads_pair, grad_query = lax.fori_loop(
        1, ctx_count, backward_turn, (key_pair, grads_pair, grad_query)
    )
    grads_pair = pass_grads(grads_pair)
    grad_query_pre = rotate(grad_query * score_scale, query_place, -1.0)
    grad_key_pre = rotate(
        grads_pair[0].reshape(micro_count, local_span, head_count, HEAD) * score_scale,
        query_place,
        -1.0,
    )
    grad_value_pre = grads_pair[1].reshape(micro_count, local_span, head_count, HEAD)
    grad_qkv_low = (
        jnp.stack([grad_query_pre, grad_key_pre, grad_value_pre], 2)
        .reshape(row_count, 3 * model_width)
        .astype(jnp.bfloat16)
    )
    _, gelu_back = jax.vjp(partial(jax.nn.gelu, approximate=True), up_proj)
    grad_up_low = gelu_back(grad_hid)[0].astype(jnp.bfloat16)
    pieces = (
        lax.all_gather(w_qkv, ("dp", "ctx"), axis=0, tiled=True),
        lax.all_gather(w_fc1, ("dp", "ctx"), axis=0, tiled=True),
    )
    term = contract_last(grad_qkv_low, pieces[0]) + contract_last(grad_up_low, pieces[1])
    _, norm_back = jax.vjp(layer_norm, inputs, gain_full, shift_full)
    grad_inputs, grad_gain_local, grad_shift_local = norm_back(term)
    token_grad = (
        (grad_out_full + grad_inputs)
        .astype(jnp.bfloat16)
        .reshape(micro_count, local_span, model_width)
    )
    vector_sums = (
        lax.psum_scatter(grad_gain_local, ("dp", "ctx"), scatter_dimension=0, tiled=True),
        lax.psum_scatter(grad_shift_local, ("dp", "ctx"), scatter_dimension=0, tiled=True),
        lax.psum_scatter(
            jnp.sum(grad_qkv_low.astype(jnp.float32), 0),
            ("dp", "ctx"),
            scatter_dimension=0,
            tiled=True,
        ),
        lax.psum_scatter(
            jnp.sum(grad_up_low.astype(jnp.float32), 0),
            ("dp", "ctx"),
            scatter_dimension=0,
            tiled=True,
        ),
        lax.psum_scatter(jnp.sum(grad_out_full, 0), ("dp", "ctx"), scatter_dimension=0, tiled=True),
    )
    joined_in = jnp.concatenate([grad_qkv_low, grad_up_low], 1)
    left = normed_low
    in_grads = lax.psum_scatter(
        contract_first(left, joined_in), ("dp", "ctx"), scatter_dimension=0, tiled=True
    )
    ratio = down_rows.shape[1] // model_width
    left = attention_low
    hidden_cols = hidden_low
    dense_term = contract_first(left, grad_out)
    down_term = contract_first(hidden_cols, grad_out).reshape(
        w_dense.shape[0] * lax.axis_size(("dp", "ctx")), ratio * model_width
    )
    out_grads = lax.psum_scatter(
        jnp.concatenate([dense_term, down_term], 1), ("dp", "ctx"), scatter_dimension=0, tiled=True
    )
    grad_w_qkv = in_grads[:, : 3 * model_width]
    grad_w_fc1 = in_grads[:, 3 * model_width :]
    grad_w_dense = out_grads[:, :model_width]
    grad_w_fc2 = out_grads[:, model_width:].reshape(w_fc2.shape)
    return (
        output,
        token_grad,
        vector_sums[0],
        vector_sums[1],
        grad_w_qkv,
        vector_sums[2],
        grad_w_dense,
        vector_sums[4],
        grad_w_fc1,
        vector_sums[3],
        grad_w_fc2,
        vector_sums[4],
    )


def solution(mesh):
    in_specs = (
        P("dp", "ctx", None),
        P("dp", None),
        P(("dp", "ctx")),
        P(("dp", "ctx")),
        P(("dp", "ctx"), None),
        P(("dp", "ctx")),
        P(("dp", "ctx"), None),
        P(("dp", "ctx")),
        P(("dp", "ctx"), None),
        P(("dp", "ctx")),
        P(("dp", "ctx"), None),
        P(("dp", "ctx")),
        P("dp", "ctx", None),
    )
    out_specs = (
        P("dp", "ctx", None),
        P("dp", "ctx", None),
        P(("dp", "ctx")),
        P(("dp", "ctx")),
        P(("dp", "ctx"), None),
        P(("dp", "ctx")),
        P(("dp", "ctx"), None),
        P(("dp", "ctx")),
        P(("dp", "ctx"), None),
        P(("dp", "ctx")),
        P(("dp", "ctx"), None),
        P(("dp", "ctx")),
    )
    return jax.shard_map(
        on_device, mesh=mesh, in_specs=in_specs, out_specs=out_specs, check_vma=False
    )
```

profile of v0, /device:TPU:1, one launch (start us, length us, event | category | flops | bytes accessed | tf_op | source)
XLA Modules:
  0.0 3770.7 jit_solution(6491535367729453203)
XLA Ops:
  14.9 42.4 %all-reduce.12 = (bf16[2048]{0:T(1024)(128)(2,1)S(1)}, bf16[2048]{0:T(1024)(128)(2,1)S(1)}, bf16[6144]{0:T(1024)(128)(2,1)S(1)}, bf16[2048]{0:T(1024)(128)(2,1)}, bf16[2048]{0:T(1024)(128)(2,1)}) all-reduce(bf16[2048]{0:T(1024)(128)(2,1)S(1)} %dynamic-update-slice.1, ...), channel_id=1, replica_groups=mesh['dp'=4,'ctx'=8] {'dp','ctx'}, use_global_device_ids=true, to_apply=%add.1 | all-reduce | flops 14336 | bytes 57344
  58.8 31.9 all-gather.8.cloned.1.call-done
  99.5 147.4 %all-gather.6.cloned.1.call-done = bf16[2048,6144]{1,0:T(8,128)(2,1)} async-done(((bf16[64,6144]{1,0:T(8,128)(2,1)}), bf16[2048,6144]{1,0:T(8,128)(2,1)}) %all-gather.6.cloned.1.call-update) | async-done | bytes 25165840 | tf_op jit(solution)/shard_map/all_gather | solution.py:101
  297.6 258.1 %while.42 = (s32[]{:T(128)}, bf16[2,2,64,2048]{3,2,1,0:T(8,128)(2,1)S(1)}, f32[2,64,32]{1,2,0:T(8,128)S(1)}, f32[2,64,32]{1,2,0:T(8,128)S(1)}, f32[2,64,32,64]{3...) while((s32[]{:T(128)}, ...), condition=%wide.region_7.8_spmd.clone, body=%wide.region_4.7_spmd.clone.sunk | while | flops 71057688 | bytes 25991652 | solution.py:160
  299.7 29.6 collective-permute-done
  372.4 33.6 collective-permute-done
  420.6 16.8 collective-permute-done
  477.7 18.7 collective-permute-done
  510.9 33.2 collective-permute-done
  576.6 326.1 %while.43 = (s32[]{:T(128)}, bf16[2,2,64,2048]{3,2,1,0:T(8,128)(2,1)S(1)}, bf16[2,2,64,2048]{3,2,1,0:T(8,128)(2,1)}, f32[2,64,32,64]{3,1,2,0:T(8,128)}, s32[]{:T...) while((s32[]{:T(128)}, ...), condition=%wide.region_10.11_spmd.clone, body=%wide.region_9.10_spmd.clone.sunk | while | flops 172237088 | bytes 60873384 | solution.py:245
  582.6 31.1 collective-permute-done.1
  905.2 48.1 %all-gather = bf16[32,1,256]{2,1,0:T(2,128)(2,1)S(1)} all-gather(bf16[1,1,256]{2,1,0:T(2,128)(2,1)S(1)} %reshape.352), channel_id=1, replica_groups=mesh['dp'=4,'ctx'=8] {'dp','ctx'}, dimensions={0}, use_global_device_ids=true | all-gather | bytes 16896 | tf_op jit(solution)/shard_map/all_gather | solution.py:90
  985.6 14.1 fusion.78
  999.7 55.2 %reshape.334 = bf16[8192,2048]{1,0:T(8,128)(2,1)} reshape(bf16[2048,8192]{1,0:T(8,128)(2,1)} %all-gather.12.cloned.1.call-done) | data formatting | bytes 67108864 | tf_op jit(solution)/shard_map/reshape | solution.py:177
  1054.8 17.5 fusion.79
  1072.4 18.4 convert_reduce_fusion.1
  1090.9 17.9 fusion.68
  1109.9 42.3 %fusion.35 = f32[2048,14336]{1,0:T(8,128)} fusion(bf16[128,2048]{1,0:T(8,128)(2,1)} %copy-done.28, bf16[128,8192]{1,0:T(8,128)(2,1)} %copy-done.25, bf16[128,6144]{1,0:T(8,128)(2,1)S(1)} %convert_element_type.210), kind=kOutput, calls=%fused_computation.60 | convolution fusion | flops 7523532800 | bytes 121634816 | tf_op jit(solution)/shard_map/dot_general | solution.py:58
  1163.0 25.6 fusion.67
  1188.7 79.3 %reshape.339 = f32[2048,8192]{1,0:T(8,128)} reshape(f32[8192,2048]{1,0:T(8,128)} %fusion.67) | data formatting | bytes 134217728 | tf_op jit(solution)/shard_map/reshape | solution.py:301
  1268.0 55.4 %pad_maximum_fusion = f32[2048,10240]{1,0:T(8,128)} fusion(f32[2048,8192]{1,0:T(8,128)} %reshape.339, f32[2048,2048]{1,0:T(8,128)} %fusion.80), kind=kLoop, calls=%fused_computation.44 | loop fusion | flops 20971520 | bytes 167772160 | tf_op jit(solution)/shard_map/concatenate | solution.py:305
  1330.5 19.9 fusion.42
  1356.4 1516.1 %all-reduce.16.cloned.1.call-done = f32[2048,14336]{1,0:T(8,128)} async-done(((f32[2048,14336]{1,0:T(8,128)}), f32[2048,14336]{1,0:T(8,128)}) %all-reduce.16.cloned.1.call-update) | async-done | bytes 117440528
  2878.6 879.2 %reduce-scatter.2.cloned.1.call-done = f32[64,10240]{1,0:T(8,128)} async-done(((f32[2048,10240]{1,0:T(8,128)}), f32[64,10240]{1,0:T(8,128)}) %reduce-scatter.2.cloned.1.call-update) | async-done | bytes 2621456 | tf_op jit(solution)/shard_map/reduce_scatter | solution.py:304
  (699 shorter events, 580.2 us)
Async XLA Ops:
  7.2 83.5 %all-gather.8.cloned.1.call-start = ((), (), s32[]{:S(2)}) async-start(), calls=%async_computation.2 | async-start | bytes 8650752 | tf_op jit(solution)/shard_map/all_gather | solution.py:168
  7.9 238.9 %all-gather.6.cloned.1.call-start = ((), (), s32[]{:S(2)}) async-start(), calls=%async_computation.1 | async-start | bytes 25952256 | tf_op jit(solution)/shard_map/all_gather | solution.py:101
  8.7 991.0 %all-gather.12.cloned.1.call-start = ((), (), s32[]{:S(2)}) async-start(), calls=%async_computation.4 | async-start | bytes 34603008 | tf_op jit(solution)/shard_map/all_gather | solution.py:169
  11.5 1060.8 %all-gather.10.cloned.1.call-start = ((), (), s32[]{:S(2)}) async-start(), calls=%async_computation.3 | async-start | bytes 34603008 | tf_op jit(solution)/shard_map/all_gather | solution.py:102
  12.1 1338.4 %all-reduce.18.cloned.1.call-start = ((), (), s32[]{:S(2)}) async-start(), calls=%async_computation.7 | async-start | bytes 163840
  297.7 31.6 collective-permute-start
  340.9 17.0 collective-permute-start
  369.4 36.6 collective-permute-start
  417.5 19.9 collective-permute-start
  474.6 21.7 collective-permute-start
  507.9 36.3 collective-permute-start
  576.8 36.9 collective-permute-start.1
  579.5 68.0 %collective-permute-start.2 = (bf16[2,2,64,2048]{3,2,1,0:T(8,128)(2,1)}, bf16[2,2,64,2048]{3,2,1,0:T(8,128)(2,1)}, u32[]{:S(2)}, u32[]{:S(2)}) collective-permute-start(bf16[2,2,64,2048]{3,2,1,0:T(8,128)(2,1)} %get-tuple-element.909), channel_id=1, source_target_pairs={{0,1},{1,2},{2,3},{3,4},{4,5},{5,6},{6,7},{7,0},{8,9},{9,10},{10,1... | collective-permute-start | bytes 3145736 | tf_op jit(solution)/shard_map/while/body/eval_jaxpr/ppermute | solution.py:19
  650.1 19.8 collective-permute-start.1
  652.5 41.9 %collective-permute-start.2 = (bf16[2,2,64,2048]{3,2,1,0:T(8,128)(2,1)}, bf16[2,2,64,2048]{3,2,1,0:T(8,128)(2,1)}, u32[]{:S(2)}, u32[]{:S(2)}) collective-permute-start(bf16[2,2,64,2048]{3,2,1,0:T(8,128)(2,1)} %get-tuple-element.909), channel_id=1, source_target_pairs={{0,1},{1,2},{2,3},{3,4},{4,5},{5,6},{6,7},{7,0},{8,9},{9,10},{10,1... | collective-permute-start | bytes 3145736 | tf_op jit(solution)/shard_map/while/body/eval_jaxpr/ppermute | solution.py:19
  699.5 36.0 collective-permute-start.2
  740.6 36.0 collective-permute-start.2
  779.3 14.2 collective-permute-start.1
  781.7 36.0 collective-permute-start.2
  822.9 36.0 collective-permute-start.2
  864.0 36.0 collective-permute-start.2
  902.7 55.5 %collective-permute-start.3 = (bf16[2,2,64,2048]{3,2,1,0:T(8,128)(2,1)}, bf16[2,2,64,2048]{3,2,1,0:T(8,128)(2,1)S(1)}, u32[]{:S(2)}, u32[]{:S(2)}) collective-permute-start(bf16[2,2,64,2048]{3,2,1,0:T(8,128)(2,1)} %get-tuple-element.505), channel_id=1, source_target_pairs={{0,1},{1,2},{2,3},{3,4},{4,5},{5,6},{6,7},{7,0},{8,9},{9,10},{10,1... | collective-permute-start | bytes 3145736 | tf_op jit(solution)/shard_map/ppermute | solution.py:19
  1109.8 1762.6 %all-reduce.16.cloned.1.call-start = ((), (), s32[]{:S(2)}) async-start(), calls=%async_computation.6 | async-start | bytes 234881024
  1152.2 2605.6 %reduce-scatter.2.cloned.1.call-start = ((), (), s32[]{:S(2)}) async-start(), calls=%async_computation.5 | async-start | bytes 86507520 | tf_op jit(solution)/shard_map/reduce_scatter | solution.py:304
  (126 other events, 4127.5 us)
Sparse Core Ops, SparseCore 0:
  10.9 79.7 all-gather.7
  93.6 153.2 all-gather.5
  249.7 219.4 all-gather.11
  471.8 226.6 all-gather.9
  1110.0 117.8 all-reduce.17
  1234.2 1638.2 all-reduce.15
  2874.9 882.8 reduce-scatter.1
where the time goes:
time: 3780 us; the launch traced here: 3770 us
  waiting for transfers between devices  2840 us (75%)
  local copies, waits for them, and re-layouts  375 us (10%)
  matrix products  296 us (8%)
  other arithmetic  107 us (3%)
  blocking collectives  90.5 us (2%)
  starting transfers between devices  50.3 us (1%)
    unnamed x9, waiting for transfers between devices  1520 us
    reduce_scatter x1, waiting for transfers between devices, on_device(): lax.psum_scatter(jnp.concatenate([dense_term, down_term], 1), ('dp', 'ctx...  879 us
    ppermute x22, waiting for transfers between devices, passed_along(): return lax.ppermute(value, axis, pairs)  259 us
    all_gather x1, waiting for transfers between devices, on_device(): lax.all_gather(w_qkv, ('dp', 'ctx'), axis=0, tiled=True)  147 us
    reshape x1, local copies, waits for them, and re-layouts, on_device(): contract_first(hidden_cols, grad_out)  79.3 us
    dot_general x3, matrix products, contract_first(): lax.dot_general(left, right, (((0,), (0,)), ((), ())), preferred_element_...  76.1 us
  transfers between devices with their start and end apart: 29, of which 19 were waited for; matrix products, arithmetic and copies ran while one was open for 19% of the time, Pallas kernels for 0%

commit v1 on v0

v1 whole, which is shorter than its diff:
```python
from functools import partial

import jax
import jax.numpy as jnp
from jax import lax
from jax.experimental import pallas as pl
from jax.experimental.pallas import tpu as pltpu
from jax.sharding import PartitionSpec as P

HEAD = 64
ROT = 32
ROPE_BASE = 10000
NORM_EPS = 1e-05
BOTH = ("dp", "ctx")
LOW = jnp.bfloat16
WIDE = jnp.float32
GELU_SCALE = 0.7978845608028654
GELU_CUBIC = 0.044715


def place(axis, index):
    return lax.dynamic_index_in_dim(axis, index, 0, keepdims=False)


class Grid:
    def __init__(self):
        self.z_count = lax.axis_size("dp")
        self.ctx_count = lax.axis_size("ctx")
        self.y_count = self.ctx_count // 4
        ctx = lax.axis_index("ctx")
        self.z = lax.axis_index("dp")
        self.y = ctx // 4
        self.x = (ctx // 2) % 2
        self.c = ctx % 2
        self.rank = self.z * self.y_count + self.y
        self.rank_count = self.z_count * self.y_count
        self.parity = (self.z + self.x) % 2

    def send(self, value, z=0, y=0, x=0, c=0):
        pairs = []
        for z_at in range(self.z_count):
            for y_at in range(self.y_count):
                for x_at in range(2):
                    for c_at in range(2):
                        z_to = (z_at + z) % self.z_count
                        y_to = (y_at + y) % self.y_count
                        source = ((z_at * self.y_count + y_at) * 2 + x_at) * 2 + c_at
                        target = ((z_to * self.y_count + y_to) * 2 + (x_at ^ x)) * 2 + (c_at ^ c)
                        pairs.append((source, target))
        return lax.ppermute(value, BOTH, pairs)


def gather_tokens(grid, value):
    own = place(value, grid.c)
    other = grid.send(place(value, 1 - grid.c), c=1)
    first = jnp.concatenate([own, other], 0)
    pieces = {0: first}
    for k in range(1, grid.z_count // 2 + 1):
        pieces[k] = grid.send(pieces[k - 1], z=1)
    for k in range(grid.z_count - 1, grid.z_count // 2, -1):
        pieces[k] = grid.send(pieces[(k + 1) % grid.z_count], z=-1)
    sequences = []
    for i in range(grid.z_count // 2):
        even, odd = pieces[2 * i], pieces[2 * i + 1]
        keep = jnp.where(grid.parity == 0, even, odd)
        away = jnp.where(grid.parity == 0, odd, even)
        parts = [keep, grid.send(away, x=1)]
        here = list(parts)
        for _ in range(1, grid.y_count):
            here = [grid.send(part, y=1) for part in here]
            parts = parts + here
        sequences.append(jnp.concatenate(parts, 0))
    return sequences


def scatter_tokens(grid, sequences):
    pieces = {}
    for i, whole in enumerate(sequences):
        halves = whole.reshape(grid.y_count, 2, -1, whole.shape[-1])
        summed = [halves[0, 0].astype(WIDE), halves[0, 1].astype(WIDE)]
        arrived = None
        for dy in range(grid.y_count - 1, 0, -1):
            step = [halves[dy, dx].astype(WIDE) for dx in range(2)]
            if arrived is not None:
                step = [a + b.astype(WIDE) for a, b in zip(step, arrived)]
            arrived = [grid.send(part.astype(LOW), y=-1) for part in step]
        summed = [a + b.astype(WIDE) for a, b in zip(summed, arrived)]
        kept = summed[0].astype(LOW)
        swapped = grid.send(summed[1].astype(LOW), x=1)
        pieces[2 * i] = jnp.where(grid.parity == 0, kept, swapped)
        pieces[2 * i + 1] = jnp.where(grid.parity == 0, swapped, kept)
    total = pieces[0].astype(WIDE)
    arrived = None
    for k in range(grid.z_count // 2, 0, -1):
        step = pieces[k] if arrived is None else (pieces[k].astype(WIDE) + arrived.astype(WIDE)).astype(LOW)
        arrived = grid.send(step, z=-1)
    total = total + arrived.astype(WIDE)
    arrived = None
    for k in range(grid.z_count // 2 + 1, grid.z_count):
        step = pieces[k] if arrived is None else (pieces[k].astype(WIDE) + arrived.astype(WIDE)).astype(LOW)
        arrived = grid.send(step, z=1)
    if arrived is not None:
        total = total + arrived.astype(WIDE)
    span = total.shape[0] // 2
    own = total[:span]
    other = grid.send(total[span:].astype(LOW), c=1).astype(WIDE)
    return jnp.where(grid.c == 0, jnp.stack([own, other]), jnp.stack([other, own]))


def gather_columns(grid, weight, parts):
    rows = weight.shape[0]
    zn, yn = grid.z_count, grid.y_count
    width = weight.shape[1] // (parts * zn * yn)
    cut = weight.reshape(rows, parts, zn, yn, width)
    by_y = jnp.zeros((yn, rows, parts, zn, width), weight.dtype)
    for dy in range(yn):
        chunk = lax.dynamic_index_in_dim(cut, (grid.y + dy) % yn, 3, keepdims=False)
        got = grid.send(chunk, y=dy) if dy else chunk
        by_y = lax.dynamic_update_index_in_dim(by_y, got, (grid.y - dy) % yn, 0)
    by_z = jnp.zeros((zn, yn, rows, parts, width), weight.dtype)
    for dz in range(zn):
        chunk = lax.dynamic_index_in_dim(by_y, (grid.z + dz) % zn, 3, keepdims=False)
        got = grid.send(chunk, z=dz) if dz else chunk
        by_z = lax.dynamic_update_index_in_dim(by_z, got, (grid.z - dz) % zn, 0)
    by_z = by_z.reshape(zn * yn, rows, parts * width)
    return gather_pairs(grid, by_z)


def gather_pairs(grid, value):
    other = grid.send(value, x=1)
    pair = jnp.where(
        grid.x == 0, jnp.stack([value, other], 1), jnp.stack([other, value], 1)
    )
    other = grid.send(pair, c=1)
    quad = jnp.where(
        grid.c == 0, jnp.stack([pair, other], 2), jnp.stack([other, pair], 2)
    )
    return quad.reshape(-1, value.shape[-1])


def scatter_pairs(grid, value):
    width = value.shape[-1]
    cut = value.reshape(-1, 2, 2, value.shape[0] // (4 * grid.group_ranks), width)
    away = lax.dynamic_index_in_dim(cut, 1 - grid.c, 2, keepdims=False).astype(LOW)
    kept = lax.dynamic_index_in_dim(cut, grid.c, 2, keepdims=False)
    cut = kept + grid.send(away, c=1).astype(WIDE)
    away = lax.dynamic_index_in_dim(cut, 1 - grid.x, 1, keepdims=False).astype(LOW)
    kept = lax.dynamic_index_in_dim(cut, grid.x, 1, keepdims=False)
    return kept + grid.send(away, x=1).astype(WIDE)


def scatter_columns(grid, value, parts):
    zn, yn = grid.z_count, grid.y_count
    grid.group_ranks = zn * yn
    summed = scatter_pairs(grid, value).astype(LOW)
    rows, width = summed.shape[1], summed.shape[2] // parts
    cut = summed.reshape(zn, yn, rows, parts, width)
    by_z = jnp.zeros((yn, rows, parts, zn, width), LOW)
    for dz in range(zn):
        chunk = place(cut, (grid.z + dz) % zn)
        got = grid.send(chunk, z=dz) if dz else chunk
        by_z = lax.dynamic_update_index_in_dim(by_z, got, (grid.z - dz) % zn, 3)
    by_y = jnp.zeros((rows, parts, zn, yn, width), LOW)
    for dy in range(yn):
        chunk = place(by_z, (grid.y + dy) % yn)
        got = grid.send(chunk, y=dy) if dy else chunk
        by_y = lax.dynamic_update_index_in_dim(by_y, got, (grid.y - dy) % yn, 3)
    return by_y.reshape(rows, -1).astype(WIDE)


def contract_last(left, right):
    return lax.dot_general(
        left, right, (((1,), (1,)), ((), ())), preferred_element_type=WIDE
    )


def contract_first(left, right):
    return lax.dot_general(
        left, right, (((0,), (0,)), ((), ())), preferred_element_type=WIDE
    )


def layer_norm(inputs, gain_vec, shift_vec):
    centre = inputs - jnp.mean(inputs, -1, keepdims=True)
    spread = jnp.mean(centre * centre, -1, keepdims=True)
    return centre * lax.rsqrt(spread + NORM_EPS) * gain_vec + shift_vec


def swap_halves(field):
    width = field.shape[-1]
    half = ROT // 2
    if width % 128 == 0:
        after = pltpu.roll(field, width - half, 1)
        before = pltpu.roll(field, half, 1)
    else:
        after = jnp.concatenate([field[:, half:], field[:, :half]], 1)
        before = jnp.concatenate([field[:, width - half :], field[:, : width - half]], 1)
    lane = lax.broadcasted_iota(jnp.int32, field.shape, 1) % HEAD
    return jnp.where(lane < half, after, before)


def attention_body(
    query_ref, key_ref, value_ref, grad_ref, cos_ref, sin_ref, column_ref, row_ref,
    mixed_ref, grad_query_ref, grad_key_ref, grad_value_ref,
):
    cosine, sine = cos_ref[...], sin_ref[...]
    scale = HEAD**-0.5
    query = query_ref[...]
    query_all = (query * cosine + swap_halves(query) * sine).astype(LOW)
    key = key_ref[...]
    key_all = (key * cosine + swap_halves(key) * sine).astype(LOW)
    value_all = value_ref[...].astype(LOW)
    grad_all = grad_ref[...]
    allowed = row_ref[...] <= column_ref[...]
    outs = []
    for at in range(query_all.shape[1] // HEAD):
        part = slice(at * HEAD, (at + 1) * HEAD)
        query_low, key_low = query_all[:, part], key_all[:, part]
        value_low, grad_low = value_all[:, part], grad_all[:, part]
        scores = jnp.where(allowed, contract_last(query_low, key_low) * scale, -1e30)
        weights = jnp.exp(scores - jnp.max(scores, -1, keepdims=True))
        probability = weights / jnp.sum(weights, -1, keepdims=True)
        probability_low = probability.astype(LOW)
        mixed = jnp.dot(probability_low, value_low, preferred_element_type=WIDE)
        delta = jnp.sum(grad_low.astype(WIDE) * mixed, -1, keepdims=True)
        grad_probability = contract_last(grad_low, value_low)
        grad_scores = (probability * (grad_probability - delta)).astype(LOW)
        grad_value = contract_first(probability_low, grad_low)
        grad_query = jnp.dot(grad_scores, key_low, preferred_element_type=WIDE) * scale
        grad_key = contract_first(grad_scores, query_low) * scale
        outs.append((mixed, grad_query, grad_key, grad_value))
    mixed, grad_query, grad_key, grad_value = [jnp.concatenate(item, 1) for item in zip(*outs)]
    mixed_ref[...] = mixed.astype(LOW)
    grad_query_ref[...] = (grad_query * cosine - swap_halves(grad_query) * sine).astype(LOW)
    grad_key_ref[...] = (grad_key * cosine - swap_halves(grad_key) * sine).astype(LOW)
    grad_value_ref[...] = grad_value.astype(LOW)


def attend(qkv, grad_attention, cosine, sine, places, length):
    tokens, width = grad_attention.shape
    lanes = min(128, width)
    block = (length, lanes)
    places = places.astype(WIDE)
    field = pl.BlockSpec(block, lambda s, h: (s, h))
    table = pl.BlockSpec(block, lambda s, h: (s, 0))
    third = lambda part: pl.BlockSpec((None, *block), lambda s, h: (part, s, h))
    low = jax.ShapeDtypeStruct((tokens, width), LOW)
    return pl.pallas_call(
        attention_body,
        grid=(tokens // length, width // lanes),
        in_specs=[
            third(0), third(1), third(2), field, table, table,
            pl.BlockSpec((length, 1), lambda s, h: (s, 0)),
            pl.BlockSpec((None, 1, length), lambda s, h: (s, 0, 0)),
        ],
        out_specs=[field] * 4,
        out_shape=[low] * 4,
        compiler_params=pltpu.CompilerParams(vmem_limit_bytes=48 * 1024 * 1024),
        cost_estimate=pl.CostEstimate(
            flops=12 * tokens * length * width, bytes_accessed=30 * tokens * width, transcendentals=tokens * length * width // HEAD
        ),
    )(
        qkv, qkv, qkv, grad_attention, cosine[:, :lanes], sine[:, :lanes],
        places[:, None], places.reshape(-1, 1, length),
    )


def rotary_tables(places):
    lane = jnp.arange(128, dtype=jnp.int32) % HEAD
    half = ROT // 2
    freqs = jnp.asarray(ROPE_BASE, WIDE) ** (-((lane % half).astype(WIDE) * (2.0 / ROT)))
    angles = places.astype(WIDE)[:, None] * freqs
    turned = (lane < ROT)[None, :]
    sign = jnp.where(lane < half, -1.0, 1.0)
    return jnp.where(turned, jnp.cos(angles), 1.0), jnp.where(turned, jnp.sin(angles) * sign, 0.0)


def on_device(
    tokens, block_order, ln_gain, ln_bias, w_qkv, b_qkv, w_dense, b_dense, w_fc1, b_fc1, w_fc2, b_fc2, cotangent,
):
    grid = Grid()
    seqs, span, model_width = tokens.shape
    device_count = grid.z_count * grid.ctx_count
    ranks = grid.rank_count
    length = span * grid.ctx_count
    block_len = span // 2
    group_seqs = grid.z_count // 2
    head_width = model_width // ranks

    vectors = (ln_gain, ln_bias, b_qkv, b_dense, b_fc1, b_fc2, block_order.astype(LOW).reshape(-1))
    sizes = [item.shape[0] for item in vectors]
    gathered = lax.all_gather(jnp.concatenate(vectors), BOTH, axis=0)
    cuts = [sum(sizes[:i]) for i in range(len(sizes) + 1)]
    gain_full, shift_full, bias_qkv, bias_dense, bias_up, bias_down = [
        gathered[:, cuts[i] : cuts[i + 1]].reshape(-1).astype(WIDE) for i in range(6)
    ]
    orders = gathered[:: grid.ctx_count, cuts[6] :].reshape(grid.z_count, 2, -1).astype(jnp.int32)

    ctx_from = jnp.stack(
        [
            (((grid.y - dy) % grid.y_count) * 2 + (grid.x ^ dx)) * 2 + (grid.c ^ dc)
            for dy in range(grid.y_count)
            for dx in range(2)
            for dc in range(2)
        ]
    )
    z_from = jnp.stack([(grid.z - 2 * i - grid.parity) % grid.z_count for i in range(group_seqs)])
    own_orders = lax.dynamic_index_in_dim(orders, grid.c, 1, keepdims=False)[z_from]
    slots = (ctx_from[:, None] * 2 + jnp.arange(2)).reshape(-1)
    places = (own_orders[:, slots][:, :, None] * block_len + jnp.arange(block_len)).reshape(-1)
    cosine, sine = rotary_tables(places)

    inputs = jnp.concatenate(gather_tokens(grid, tokens), 0)
    win_qkv = gather_columns(grid, w_qkv, 3)
    win_up = gather_columns(grid, w_fc1, 1)
    grad_out = jnp.concatenate(gather_tokens(grid, cotangent), 0)
    wout_dense = gather_pairs(grid, w_dense[None])
    wout_down = gather_pairs(grid, w_fc2[None])

    normed_low = layer_norm(inputs.astype(WIDE), gain_full, shift_full).astype(LOW)
    own_bias_qkv = lax.dynamic_index_in_dim(bias_qkv.reshape(3, ranks, -1), grid.rank, 1, keepdims=False)
    own_bias_up = place(bias_up.reshape(ranks, -1), grid.rank)
    qkv = jnp.stack(
        [
            jnp.dot(normed_low, win_qkv[:, i * head_width : (i + 1) * head_width], preferred_element_type=WIDE)
            + own_bias_qkv[i]
            for i in range(3)
        ]
    )
    grad_attention_low = contract_last(grad_out, wout_dense).astype(LOW)
    attention_low, grad_query_low, grad_key_low, grad_value_low = attend(
        qkv, grad_attention_low, cosine, sine, places, length
    )
    grad_qkv_low = jnp.concatenate([grad_query_low, grad_key_low, grad_value_low], 1)

    up = jnp.dot(normed_low, win_up, preferred_element_type=WIDE) + own_bias_up
    bent = jnp.tanh(GELU_SCALE * (up + GELU_CUBIC * up * up * up))
    hidden_low = (0.5 * up * (1.0 + bent)).astype(LOW)
    slope = 0.5 * (1.0 + bent) + 0.5 * up * (1.0 - bent * bent) * GELU_SCALE * (1.0 + 3.0 * GELU_CUBIC * up * up)
    grad_up_low = (contract_last(grad_out, wout_down) * slope).astype(LOW)

    projected = (
        jnp.dot(attention_low, wout_dense, preferred_element_type=WIDE)
        + jnp.dot(hidden_low, wout_down, preferred_element_type=WIDE)
    ).astype(LOW)
    projected = scatter_tokens(grid, [projected[i * length : (i + 1) * length] for i in range(group_seqs)])
    own_inputs = tokens.astype(WIDE)
    output = (own_inputs + projected + bias_dense + bias_down).astype(LOW)

    grad_normed = (contract_last(grad_qkv_low, win_qkv) + contract_last(grad_up_low, win_up)).astype(LOW)
    grad_normed = scatter_tokens(grid, [grad_normed[i * length : (i + 1) * length] for i in range(group_seqs)])

    centre = own_inputs - jnp.mean(own_inputs, -1, keepdims=True)
    turn = lax.rsqrt(jnp.mean(centre * centre, -1, keepdims=True) + NORM_EPS)
    unit = centre * turn
    scaled = grad_normed * gain_full
    own_grad = cotangent.astype(WIDE)
    token_grad = (
        own_grad
        + turn * (scaled - jnp.mean(scaled, -1, keepdims=True) - unit * jnp.mean(scaled * unit, -1, keepdims=True))
    ).astype(LOW)

    def laid(part, count):
        whole = jnp.zeros((count, ranks, part.shape[-1]), WIDE)
        whole = lax.dynamic_update_index_in_dim(whole, part, grid.rank, 1)
        return whole.reshape(device_count, -1)

    sums = jnp.concatenate(
        [
            jnp.sum(grad_normed * unit, (0, 1)).reshape(device_count, -1),
            jnp.sum(grad_normed, (0, 1)).reshape(device_count, -1),
            laid(jnp.sum(grad_qkv_low.astype(WIDE), 0).reshape(3, -1), 3),
            jnp.sum(own_grad, (0, 1)).reshape(device_count, -1),
            laid(jnp.sum(grad_up_low.astype(WIDE), 0).reshape(1, -1), 1),
        ],
        1,
    )
    sums = lax.psum_scatter(sums, BOTH, scatter_dimension=0, tiled=False)
    grad_gain, grad_shift = sums[: sizes[0]], sums[sizes[0] : 2 * sizes[0]]
    rest = sums[2 * sizes[0] :]
    grad_bias_qkv = rest[: sizes[2]]
    grad_bias_out = rest[sizes[2] : sizes[2] + sizes[3]]
    grad_bias_up = rest[sizes[2] + sizes[3] :]

    grid.group_ranks = 1
    grad_w_dense = scatter_pairs(grid, contract_first(attention_low, grad_out))[0]
    grad_w_down = scatter_pairs(grid, contract_first(hidden_low, grad_out))[0]
    grad_w_up = scatter_columns(grid, contract_first(normed_low, grad_up_low), 1)
    grad_w_qkv = scatter_columns(grid, contract_first(normed_low, grad_qkv_low), 3)
    return (
        output, token_grad, grad_gain, grad_shift, grad_w_qkv, grad_bias_qkv,
        grad_w_dense, grad_bias_out, grad_w_up, grad_bias_up, grad_w_down, grad_bias_out,
    )


def solution(mesh):
    rows = P(("dp", "ctx"), None)
    vector = P(("dp", "ctx"))
    spread = P("dp", "ctx", None)
    in_specs = (
        spread, P("dp", None), vector, vector, rows, vector, rows, vector, rows, vector, rows, vector, spread,
    )
    out_specs = (
        spread, spread, vector, vector, rows, vector, rows, vector, rows, vector, rows, vector,
    )
    return jax.shard_map(on_device, mesh=mesh, in_specs=in_specs, out_specs=out_specs, check_vma=False)
```

time: 3780 us -> 837 us (0.22)
  waiting for transfers between devices: 2840 us -> 351 us
  local copies, waits for them, and re-layouts: 375 us -> 133 us
  matrix products: 296 us -> 65.3 us
  starting transfers between devices: 50.3 us -> 109 us
  blocking collectives: 90.5 us -> 46.8 us
    unnamed x9 -> x2, waiting for transfers between devices: 1520 us -> 99.2 us
    reduce_scatter x1 -> x0, waiting for transfers between devices: 879 us -> none  [on_device(): lax.psum_scatter(jnp.concatenate([dense_term, down_term], 1), ('dp', 'ctx...]
    all_gather x4 -> x0, waiting for transfers between devices: 179 us -> none  [the longest x1 147 us: on_device(): lax.all_gather(w_qkv, ('dp', 'ctx'), axis=0, tiled=True)]
    reshape x21 -> x10, local copies, waits for them, and re-layouts: 179 us -> 7.93 us  [the longest x2 3.36 us: gather_columns(): cut = weight.reshape(rows, parts, zn, yn, width)]
    dot_general x59 -> x6, matrix products: 164 us -> 16.6 us  [the longest x1 6.96 us: on_device(): jnp.dot(hidden_low, wout_down, preferred_element_type=WIDE)]
    ppermute x22 -> x72, starting transfers between devices: 50.1 us -> 109 us  [send(): return lax.ppermute(value, BOTH, pairs)]
    concatenate x2, other arithmetic: 56.4 us -> 3.74 us  [gather_tokens(): first = jnp.concatenate([own, other], 0)]
    dynamic_update_slice x0 -> x26, local copies, waits for them, and re-layouts: none -> 52.6 us  [the longest x4 42.2 us: scatter_columns(): by_y = lax.dynamic_update_index_in_dim(by_y, got, (grid.y - dy) % yn, 3)]
  transfers between devices with their start and end apart: 29 -> 73, of which waited for: 19 -> 31; matrix products, arithmetic and copies ran while one was open for 19% -> 31% of each run, Pallas kernels for 0% -> 2%
where the time goes in v1:
time: 837 us; the launch traced here: 821 us
  waiting for transfers between devices  351 us (42%)
  local copies, waits for them, and re-layouts  133 us (16%)
  starting transfers between devices  109 us (13%)
  other arithmetic  80 us (10%)
  matrix products  65.3 us (8%)
  blocking collectives  46.8 us (6%)
  Pallas kernels  20.2 us (2%)
  between operations  16.1 us (2%)
    ppermute x72, waiting for transfers between devices, send(): return lax.ppermute(value, BOTH, pairs)  252 us
    ppermute x72, starting transfers between devices, send(): return lax.ppermute(value, BOTH, pairs)  109 us
    unnamed x2, waiting for transfers between devices  99.2 us
    unnamed x1, blocking collectives  46.8 us
    dynamic_update_slice x4, local copies, waits for them, and re-layouts, scatter_columns(): by_y = lax.dynamic_update_index_in_dim(by_y, got, (grid.y - dy) % yn, 3)  42.2 us
    dot_general x4, matrix products, contract_first(): lax.dot_general(left, right, (((0,), (0,)), ((), ())), preferred_element_...  26.3 us
    dot_general x4, matrix products, contract_last(): lax.dot_general(left, right, (((1,), (1,)), ((), ())), preferred_element_...  22.4 us
    pallas_call x1, Pallas kernels, attend(): pl.pallas_call(attention_body, grid=(tokens // length, width // lanes), i...  20.2 us
  transfers between devices with their start and end apart: 73, of which 31 were waited for; matrix products, arithmetic and copies ran while one was open for 31% of the time, Pallas kernels for 2%

profile of v1, /device:TPU:1, one launch (start us, length us, event | category | flops | bytes accessed | tf_op | source)
XLA Modules:
  0.0 821.2 jit_solution(13991494937077492759)
XLA Ops:
  26.2 46.8 %all-reduce = bf16[23552]{0:T(1024)(128)(2,1)S(1)} all-reduce(bf16[23552]{0:T(1024)(128)(2,1)S(1)} %dynamic-update-slice), channel_id=2, replica_groups=mesh['dp'=4,'ctx'=8] {'dp','ctx'}, use_global_device_ids=true, to_apply=%add | all-reduce | flops 23552 | bytes 94208
  105.4 8.9 %collective-permute-done.11 = bf16[2,64,3,256]{3,1,2,0:T(8,128)(2,1)S(1)} collective-permute-done((bf16[2,64,3,256]{3,1,2,0:T(8,128)(2,1)S(1)}, bf16[2,64,3,256]{3,1,2,0:T(8,128)(2,1)S(1)}, u32[]{:S(2)}, u32[]{:S(2)}) %collective-permute-start.11) | collective-permute-done | bytes 196640 | tf_op jit(solution)/shard_map/ppermute | solution.py:50
  115.5 10.2 %collective-permute-done.12 = bf16[2,64,3,256]{3,1,2,0:T(8,128)(2,1)S(1)} collective-permute-done((bf16[2,64,3,256]{3,1,2,0:T(8,128)(2,1)S(1)}, bf16[2,64,3,256]{3,1,2,0:T(8,128)(2,1)S(1)}, u32[]{:S(2)}, u32[]{:S(2)}) %collective-permute-start.12) | collective-permute-done | bytes 196640 | tf_op jit(solution)/shard_map/ppermute | solution.py:50
  144.5 9.6 %collective-permute-done.30 = bf16[2,64,1,1024]{3,1,0,2:T(8,128)(2,1)S(1)} collective-permute-done((bf16[2,64,1,1024]{3,1,0,2:T(8,128)(2,1)}, bf16[2,64,1,1024]{3,1,0,2:T(8,128)(2,1)S(1)}, u32[]{:S(2)}, u32[]{:S(2)}) %collective-permute-start.30) | collective-permute-done | bytes 262176 | tf_op jit(solution)/shard_map/ppermute | solution.py:50
  162.1 8.6 %collective-permute-done.17 = bf16[128,2048]{1,0:T(8,128)(2,1)S(1)} collective-permute-done((bf16[128,2048]{1,0:T(8,128)(2,1)}, bf16[128,2048]{1,0:T(8,128)(2,1)S(1)}, u32[]{:S(2)}, u32[]{:S(2)}) %collective-permute-start.17) | collective-permute-done | bytes 524320 | tf_op jit(solution)/shard_map/ppermute | solution.py:50
  197.7 15.6 %collective-permute-start.5 = (bf16[128,2048]{1,0:T(8,128)(2,1)}, bf16[128,2048]{1,0:T(8,128)(2,1)S(1)}, u32[]{:S(2)}, u32[]{:S(2)}) collective-permute-start(bf16[128,2048]{1,0:T(8,128)(2,1)} %collective-permute-done.1), channel_id=1, source_target_pairs={{0,8},{1,9},{2,10},{3,11},{4,12},{5,13},{6,14},{7,15},{8,16},{9,17... | collective-permute-start | bytes 1572872 | tf_op jit(solution)/shard_map/ppermute | solution.py:50
  215.5 9.6 %collective-permute-done.4 = bf16[128,2048]{1,0:T(8,128)(2,1)S(1)} collective-permute-done((bf16[128,2048]{1,0:T(8,128)(2,1)S(1)}, bf16[128,2048]{1,0:T(8,128)(2,1)S(1)}, u32[]{:S(2)}, u32[]{:S(2)}) %collective-permute-start.4) | collective-permute-done | bytes 524320 | tf_op jit(solution)/shard_map/ppermute | solution.py:50
  225.4 10.9 %collective-permute-done.20 = bf16[128,2048]{1,0:T(8,128)(2,1)S(1)} collective-permute-done((bf16[128,2048]{1,0:T(8,128)(2,1)S(1)}, bf16[128,2048]{1,0:T(8,128)(2,1)S(1)}, u32[]{:S(2)}, u32[]{:S(2)}) %collective-permute-start.20) | collective-permute-done | bytes 524320 | tf_op jit(solution)/shard_map/ppermute | solution.py:50
  279.5 9.3 %collective-permute-done.25 = bf16[128,2048]{1,0:T(8,128)(2,1)S(1)} collective-permute-done((bf16[128,2048]{1,0:T(8,128)(2,1)S(1)}, bf16[128,2048]{1,0:T(8,128)(2,1)S(1)}, u32[]{:S(2)}, u32[]{:S(2)}) %collective-permute-start.25) | collective-permute-done | bytes 524320 | tf_op jit(solution)/shard_map/ppermute | solution.py:50
  300.6 20.2 %shard_map.220 = (bf16[1024,256]{1,0:T(8,128)(2,1)S(1)}, bf16[1024,256]{1,0:T(8,128)(2,1)S(1)}, bf16[1024,256]{1,0:T(8,128)(2,1)S(1)}, bf16[1024,256]{1,0:T(8,128)(2,1)S(1)}) custom-call(f32[3,1024,256]{2,1,0:T(8,128)} %pad_maximum_fusion.query_ref.key_ref.value_ref, f32[3,1024,256]{2,1,0:T(8,128)} %pad_maximum_fusion.query_ref.key_ref.value_ref, ...), custom_call_target="tpu_custom_call" | custom-call | flops 1610612736 | bytes 7864320 | tf_op jit(solution)/shard_map/pallas_call | solution.py:248
  330.4 8.1 collective-permute-start.56
  380.7 10.6 %fusion.64 = f32[1024,2048]{1,0:T(8,128)} fusion(bf16[1024,2048]{1,0:T(8,128)(2,1)S(1)} %copy-done.32, f32[1024,1024]{1,0:T(8,128)} %copy-done.46, f32[1024]{0:T(1024)S(1)} %bitcast.382), kind=kOutput, calls=%fused_computation.275 | convolution fusion | flops 4305453056 | bytes 16781312 | tf_op jit(solution)/shard_map/dot_general | solution.py:178
  398.2 8.4 %add_convert_fusion = bf16[1024,2048]{1,0:T(8,128)(2,1)} fusion(f32[1024,2048]{1,0:T(8,128)} %fusion.69, bf16[1024,1024]{1,0:T(8,128)(2,1)S(1)} %get-tuple-element.96, bf16[2048,1024]{1,0:T(8,128)(2,1)S(1)} %bitcast.359), kind=kOutput, calls=%fused_computation.10 | convolution fusion | flops 4299161600 | bytes 18874368 | tf_op jit(solution)/shard_map/dot_general | solution.py:172
  429.2 16.1 %collective-permute-done.47 = bf16[128,2048]{1,0:T(8,128)(2,1)} collective-permute-done((bf16[128,2048]{1,0:T(8,128)(2,1)}, bf16[128,2048]{1,0:T(8,128)(2,1)}, u32[]{:S(2)}, u32[]{:S(2)}) %collective-permute-start.47) | collective-permute-done | bytes 524320 | tf_op jit(solution)/shard_map/ppermute | solution.py:50
  448.3 19.3 %collective-permute-done.40 = bf16[128,2048]{1,0:T(8,128)(2,1)S(1)} collective-permute-done((bf16[128,2048]{1,0:T(8,128)(2,1)}, bf16[128,2048]{1,0:T(8,128)(2,1)S(1)}, u32[]{:S(2)}, u32[]{:S(2)}) %collective-permute-start.40) | collective-permute-done | bytes 524320 | tf_op jit(solution)/shard_map/ppermute | solution.py:50
  469.9 9.0 %collective-permute-done.37 = bf16[128,2048]{1,0:T(8,128)(2,1)S(1)} collective-permute-done((bf16[128,2048]{1,0:T(8,128)(2,1)S(1)}, bf16[128,2048]{1,0:T(8,128)(2,1)S(1)}, u32[]{:S(2)}, u32[]{:S(2)}) %collective-permute-start.37) | collective-permute-done | bytes 524320 | tf_op jit(solution)/shard_map/ppermute | solution.py:50
  502.4 14.1 %collective-permute-done.57 = bf16[8,64,768]{2,1,0:T(8,128)(2,1)S(1)} collective-permute-done((bf16[8,64,768]{2,1,0:T(8,128)(2,1)S(1)}, bf16[8,64,768]{2,1,0:T(8,128)(2,1)S(1)}, u32[]{:S(2)}, u32[]{:S(2)}) %collective-permute-start.57) | collective-permute-done | bytes 786464 | tf_op jit(solution)/shard_map/ppermute | solution.py:50
  531.8 19.2 %collective-permute-done.58 = bf16[2,64,3,256]{3,1,2,0:T(8,128)(2,1)S(1)} collective-permute-done((bf16[2,64,3,256]{3,1,2,0:T(8,128)(2,1)S(1)}, bf16[2,64,3,256]{3,1,2,0:T(8,128)(2,1)S(1)}, u32[]{:S(2)}, u32[]{:S(2)}) %collective-permute-start.58) | collective-permute-done | bytes 196640 | tf_op jit(solution)/shard_map/ppermute | solution.py:50
  551.0 10.4 %collective-permute-done.59 = bf16[2,64,3,256]{3,1,2,0:T(8,128)(2,1)S(1)} collective-permute-done((bf16[2,64,3,256]{3,1,2,0:T(8,128)(2,1)S(1)}, bf16[2,64,3,256]{3,1,2,0:T(8,128)(2,1)S(1)}, u32[]{:S(2)}, u32[]{:S(2)}) %collective-permute-start.59) | collective-permute-done | bytes 196640 | tf_op jit(solution)/shard_map/ppermute | solution.py:50
  584.6 14.3 %dynamic_update_slice.106 = bf16[64,3,4,2,256]{4,3,2,1,0:T(2,128)(2,1)} dynamic-update-slice(bf16[64,3,4,2,256]{4,3,2,1,0:T(2,128)(2,1)} %broadcast_in_dim.188, bf16[64,3,4,1,256]{4,3,2,1,0:T(2,128)(2,1)S(1)} %copy.112, s32[]{:T(128)} %constant.460.clone.1, s32[]{:T(128)} %constant.460.clone.1, s32[]{:T(128)} %constant.460.clone.1, s32[]{:T(128)S(6)} %select_n.606, s32[]{:T(128)} %constant.460.clone.1) | dynamic-update-slice | bytes 786436 | tf_op jit(solution)/shard_map/jit(dynamic_update_index_in_dim)/dynamic_update_slice | solution.py:167
  601.4 14.3 %dynamic_update_slice.107 = bf16[64,3,4,2,256]{4,3,2,1,0:T(2,128)(2,1)} dynamic-update-slice(bf16[64,3,4,2,256]{4,3,2,1,0:T(2,128)(2,1)} %dynamic_update_slice.106, bf16[64,3,4,1,256]{4,3,2,1,0:T(2,128)(2,1)S(1)} %copy.113, s32[]{:T(128)} %constant.460.clone.1, s32[]{:T(128)} %constant.460.clone.1, s32[]{:T(128)} %constant.460.clone.1, s32[]{:T(128)S(6)} %select_n.610, s32[]{:T(128)} %constant.460.clone.1) | dynamic-update-slice | bytes 786436 | tf_op jit(solution)/shard_map/jit(dynamic_update_index_in_dim)/dynamic_update_slice | solution.py:167
  649.6 16.7 %collective-permute-done.65 = bf16[8,64,1024]{2,1,0:T(8,128)(2,1)} collective-permute-done((bf16[8,64,1024]{2,1,0:T(8,128)(2,1)}, bf16[8,64,1024]{2,1,0:T(8,128)(2,1)}, u32[]{:S(2)}, u32[]{:S(2)}) %collective-permute-start.65) | collective-permute-done | bytes 1048608 | tf_op jit(solution)/shard_map/ppermute | solution.py:50
  671.8 99.1 %all-reduce.4.cloned.1.call-done = f32[32,640]{1,0:T(8,128)} async-done(((f32[32,640]{1,0:T(8,128)}), f32[32,640]{1,0:T(8,128)}) %all-reduce.4.cloned.1.call-update) | async-done | bytes 81936
  778.2 11.5 %collective-permute-done.67 = bf16[2,64,1,1024]{3,1,0,2:T(8,128)(2,1)S(1)} collective-permute-done((bf16[2,64,1,1024]{3,1,0,2:T(8,128)(2,1)}, bf16[2,64,1,1024]{3,1,0,2:T(8,128)(2,1)S(1)}, u32[]{:S(2)}, u32[]{:S(2)}) %collective-permute-start.67) | collective-permute-done | bytes 262176 | tf_op jit(solution)/shard_map/ppermute | solution.py:50
  (444 shorter events, 384.2 us)
Async XLA Ops:
  7.2 763.7 %all-reduce.4.cloned.1.call-start = ((), (), s32[]{:S(2)}) async-start(), calls=%async_computation | async-start | bytes 163840
  9.2 73.7 %collective-permute-start = (bf16[64,2048]{1,0:T(8,128)(2,1)}, bf16[64,2048]{1,0:T(8,128)(2,1)}, u32[]{:S(2)}, u32[]{:S(2)}) collective-permute-start(bf16[64,2048]{1,0:T(8,128)(2,1)} %get-tuple-element.82), channel_id=1, source_target_pairs={{0,1},{1,0},{2,3},{3,2},{4,5},{5,4},{6,7},{7,6},{8,9},{9,8},{10,11... | collective-permute-start | bytes 786440 | tf_op jit(solution)/shard_map/ppermute | solution.py:50
  15.3 80.1 %collective-permute-start.10 = (bf16[64,3,4,256]{3,0,2,1:T(8,128)(2,1)}, bf16[64,3,4,256]{3,0,2,1:T(8,128)(2,1)}, u32[]{:S(2)}, u32[]{:S(2)}) collective-permute-start(bf16[64,3,4,256]{3,0,2,1:T(8,128)(2,1)} %bitcast.325), channel_id=1, source_target_pairs={{0,4},{1,5},{2,6},{3,7},{4,0},{5,1},{6,2},{7,3},{8,12},{9,13},{10,... | collective-permute-start | bytes 1179656 | tf_op jit(solution)/shard_map/ppermute | solution.py:50
  18.8 71.5 %collective-permute-start.16 = (bf16[64,2048]{1,0:T(8,128)(2,1)}, bf16[64,2048]{1,0:T(8,128)(2,1)}, u32[]{:S(2)}, u32[]{:S(2)}) collective-permute-start(bf16[64,2048]{1,0:T(8,128)(2,1)} %get-tuple-element.80), channel_id=1, source_target_pairs={{0,1},{1,0},{2,3},{3,2},{4,5},{5,4},{6,7},{7,6},{8,9},{9,8},{10,11... | collective-permute-start | bytes 786440 | tf_op jit(solution)/shard_map/ppermute | solution.py:50
  19.1 67.0 %collective-permute-start.26 = (bf16[1,64,2048]{2,1,0:T(8,128)(2,1)}, bf16[1,64,2048]{2,1,0:T(8,128)(2,1)}, u32[]{:S(2)}, u32[]{:S(2)}) collective-permute-start(bf16[1,64,2048]{2,1,0:T(8,128)(2,1)} %bitcast.25), channel_id=1, source_target_pairs={{0,2},{1,3},{2,0},{3,1},{4,6},{5,7},{6,4},{7,5},{8,10},{9,11},{10,... | collective-permute-start | bytes 786440 | tf_op jit(solution)/shard_map/ppermute | solution.py:50
  25.3 74.6 %collective-permute-start.28 = (bf16[64,1,4,1024]{3,0,2,1:T(8,128)(2,1)}, bf16[64,1,4,1024]{3,0,2,1:T(8,128)(2,1)}, u32[]{:S(2)}, u32[]{:S(2)}) collective-permute-start(bf16[64,1,4,1024]{3,0,2,1:T(8,128)(2,1)} %bitcast.324), channel_id=1, source_target_pairs={{0,4},{1,5},{2,6},{3,7},{4,0},{5,1},{6,2},{7,3},{8,12},{9,13},{10,... | collective-permute-start | bytes 1572872 | tf_op jit(solution)/shard_map/ppermute | solution.py:50
  83.0 90.0 %collective-permute-start.34 = (bf16[1,256,2048]{2,1,0:T(8,128)(2,1)}, bf16[1,256,2048]{2,1,0:T(8,128)(2,1)}, u32[]{:S(2)}, u32[]{:S(2)}) collective-permute-start(bf16[1,256,2048]{2,1,0:T(8,128)(2,1)} %bitcast.70), channel_id=1, source_target_pairs={{0,2},{1,3},{2,0},{3,1},{4,6},{5,7},{6,4},{7,5},{8,10},{9,11},{10,... | collective-permute-start | bytes 3145736 | tf_op jit(solution)/shard_map/ppermute | solution.py:50
  90.3 146.1 %collective-permute-start.6 = (bf16[128,2048]{1,0:T(8,128)(2,1)}, bf16[128,2048]{1,0:T(8,128)(2,1)}, u32[]{:S(2)}, u32[]{:S(2)}) collective-permute-start(bf16[128,2048]{1,0:T(8,128)(2,1)} %pad_maximum_fusion.3), channel_id=1, source_target_pairs={{0,24},{1,25},{2,26},{3,27},{4,28},{5,29},{6,30},{7,31},{8,0},{9,1... | collective-permute-start | bytes 1572872 | tf_op jit(solution)/shard_map/ppermute | solution.py:50
  95.4 64.1 %collective-permute-start.27 = (bf16[1,2,64,2048]{3,2,1,0:T(8,128)(2,1)}, bf16[1,2,64,2048]{3,2,1,0:T(8,128)(2,1)}, u32[]{:S(2)}, u32[]{:S(2)}) collective-permute-start(bf16[1,2,64,2048]{3,2,1,0:T(8,128)(2,1)} %maximum_select_fusion.12), channel_id=1, source_target_pairs={{0,1},{1,0},{2,3},{3,2},{4,5},{5,4},{6,7},{7,6},{8,9},{9,8},{10,11... | collective-permute-start | bytes 1572872 | tf_op jit(solution)/shard_map/ppermute | solution.py:50
  158.5 56.0 %collective-permute-start.14 = (bf16[8,64,768]{2,1,0:T(8,128)(2,1)}, bf16[8,64,768]{2,1,0:T(8,128)(2,1)S(1)}, u32[]{:S(2)}, u32[]{:S(2)}) collective-permute-start(bf16[8,64,768]{2,1,0:T(8,128)(2,1)} %reshape.1018), channel_id=1, source_target_pairs={{0,2},{1,3},{2,0},{3,1},{4,6},{5,7},{6,4},{7,5},{8,10},{9,11},{10,... | collective-permute-start | bytes 2359304 | tf_op jit(solution)/shard_map/ppermute | solution.py:50
  236.4 112.2 %collective-permute-start.35 = (bf16[1,2,256,2048]{3,2,1,0:T(8,128)(2,1)}, bf16[1,2,256,2048]{3,2,1,0:T(8,128)(2,1)}, u32[]{:S(2)}, u32[]{:S(2)}) collective-permute-start(bf16[1,2,256,2048]{3,2,1,0:T(8,128)(2,1)} %maximum_select_fusion.5), channel_id=1, source_target_pairs={{0,1},{1,0},{2,3},{3,2},{4,5},{5,4},{6,7},{7,6},{8,9},{9,8},{10,11... | collective-permute-start | bytes 6291464 | tf_op jit(solution)/shard_map/ppermute | solution.py:50
  239.4 54.7 %collective-permute-start.15 = (bf16[8,2,64,768]{3,2,0,1:T(8,128)(2,1)S(1)}, bf16[8,2,64,768]{3,2,0,1:T(8,128)(2,1)S(1)}, u32[]{:S(2)}, u32[]{:S(2)}) collective-permute-start(bf16[8,2,64,768]{3,2,0,1:T(8,128)(2,1)S(1)} %maximum_select_fusion.7), channel_id=1, source_target_pairs={{0,1},{1,0},{2,3},{3,2},{4,5},{5,4},{6,7},{7,6},{8,9},{9,8},{10,11... | collective-permute-start | bytes 4718600 | tf_op jit(solution)/shard_map/ppermute | solution.py:50
  267.3 89.3 %collective-permute-start.33 = (bf16[8,2,64,1024]{3,2,1,0:T(8,128)(2,1)}, bf16[8,2,64,1024]{3,2,1,0:T(8,128)(2,1)}, u32[]{:S(2)}, u32[]{:S(2)}) collective-permute-start(bf16[8,2,64,1024]{3,2,1,0:T(8,128)(2,1)} %maximum_select_fusion.3), channel_id=1, source_target_pairs={{0,1},{1,0},{2,3},{3,2},{4,5},{5,4},{6,7},{7,6},{8,9},{9,8},{10,11... | collective-permute-start | bytes 6291464 | tf_op jit(solution)/shard_map/ppermute | solution.py:50
  330.4 150.7 %collective-permute-start.56 = (bf16[8,2,64,768]{3,2,0,1:T(8,128)(2,1)}, bf16[8,2,64,768]{3,2,0,1:T(8,128)(2,1)}, u32[]{:S(2)}, u32[]{:S(2)}) collective-permute-start(bf16[8,2,64,768]{3,2,0,1:T(8,128)(2,1)} %fusion.17), channel_id=1, source_target_pairs={{0,1},{1,0},{2,3},{3,2},{4,5},{5,4},{6,7},{7,6},{8,9},{9,8},{10,11... | collective-permute-start | bytes 4718600 | tf_op jit(solution)/shard_map/ppermute | solution.py:50
  411.3 73.8 %collective-permute-start.49 = (bf16[128,2048]{1,0:T(8,128)(2,1)}, bf16[128,2048]{1,0:T(8,128)(2,1)}, u32[]{:S(2)}, u32[]{:S(2)}) collective-permute-start(bf16[128,2048]{1,0:T(8,128)(2,1)} %get-tuple-element.41), channel_id=1, source_target_pairs={{0,4},{1,5},{2,6},{3,7},{4,0},{5,1},{6,2},{7,3},{8,12},{9,13},{10,... | collective-permute-start | bytes 1572872 | tf_op jit(solution)/shard_map/ppermute | solution.py:50
  413.8 107.0 %collective-permute-start.46 = (bf16[128,2048]{1,0:T(8,128)(2,1)}, bf16[128,2048]{1,0:T(8,128)(2,1)}, u32[]{:S(2)}, u32[]{:S(2)}) collective-permute-start(bf16[128,2048]{1,0:T(8,128)(2,1)} %get-tuple-element.39), channel_id=1, source_target_pairs={{0,4},{1,5},{2,6},{3,7},{4,0},{5,1},{6,2},{7,3},{8,12},{9,13},{10,... | collective-permute-start | bytes 1572872 | tf_op jit(solution)/shard_map/ppermute | solution.py:50
  485.1 87.2 %collective-permute-start.36 = (bf16[128,2048]{1,0:T(8,128)(2,1)}, bf16[128,2048]{1,0:T(8,128)(2,1)}, u32[]{:S(2)}, u32[]{:S(2)}) collective-permute-start(bf16[128,2048]{1,0:T(8,128)(2,1)} %get-tuple-element.43), channel_id=1, source_target_pairs={{0,4},{1,5},{2,6},{3,7},{4,0},{5,1},{6,2},{7,3},{8,12},{9,13},{10,... | collective-permute-start | bytes 1572872 | tf_op jit(solution)/shard_map/ppermute | solution.py:50
  499.8 79.3 %collective-permute-start.38 = (bf16[128,2048]{1,0:T(8,128)(2,1)}, bf16[128,2048]{1,0:T(8,128)(2,1)}, u32[]{:S(2)}, u32[]{:S(2)}) collective-permute-start(bf16[128,2048]{1,0:T(8,128)(2,1)} %fusion.47), channel_id=1, source_target_pairs={{0,2},{1,3},{2,0},{3,1},{4,6},{5,7},{6,4},{7,5},{8,10},{9,11},{10,... | collective-permute-start | bytes 1572872 | tf_op jit(solution)/shard_map/ppermute | solution.py:50
  520.8 98.1 %collective-permute-start.54 = (bf16[128,2048]{1,0:T(8,128)(2,1)}, bf16[128,2048]{1,0:T(8,128)(2,1)}, u32[]{:S(2)}, u32[]{:S(2)}) collective-permute-start(bf16[128,2048]{1,0:T(8,128)(2,1)} %get-tuple-element.36), channel_id=1, source_target_pairs={{0,8},{1,9},{2,10},{3,11},{4,12},{5,13},{6,14},{7,15},{8,16},{9,17... | collective-permute-start | bytes 1572872 | tf_op jit(solution)/shard_map/ppermute | solution.py:50
  567.8 53.5 %collective-permute-start.53 = (bf16[128,2048]{1,0:T(8,128)(2,1)}, bf16[128,2048]{1,0:T(8,128)(2,1)}, u32[]{:S(2)}, u32[]{:S(2)}) collective-permute-start(bf16[128,2048]{1,0:T(8,128)(2,1)} %add_convert_fusion.2), channel_id=1, source_target_pairs={{0,24},{1,25},{2,26},{3,27},{4,28},{5,29},{6,30},{7,31},{8,0},{9,1... | collective-permute-start | bytes 1572872 | tf_op jit(solution)/shard_map/ppermute | solution.py:50
  572.3 63.7 %collective-permute-start.64 = (bf16[8,2,64,1024]{3,2,1,0:T(8,128)(2,1)}, bf16[8,2,64,1024]{3,2,1,0:T(8,128)(2,1)}, u32[]{:S(2)}, u32[]{:S(2)}) collective-permute-start(bf16[8,2,64,1024]{3,2,1,0:T(8,128)(2,1)} %fusion.13), channel_id=1, source_target_pairs={{0,1},{1,0},{2,3},{3,2},{4,5},{5,4},{6,7},{7,6},{8,9},{9,8},{10,11... | collective-permute-start | bytes 6291464 | tf_op jit(solution)/shard_map/ppermute | solution.py:50
  579.0 62.5 %collective-permute-start.70 = (bf16[1,2,256,2048]{3,2,1,0:T(8,128)(2,1)}, bf16[1,2,256,2048]{3,2,1,0:T(8,128)(2,1)}, u32[]{:S(2)}, u32[]{:S(2)}) collective-permute-start(bf16[1,2,256,2048]{3,2,1,0:T(8,128)(2,1)} %fusion.14), channel_id=1, source_target_pairs={{0,1},{1,0},{2,3},{3,2},{4,5},{5,4},{6,7},{7,6},{8,9},{9,8},{10,11... | collective-permute-start | bytes 6291464 | tf_op jit(solution)/shard_map/ppermute | solution.py:50
  669.5 107.8 %collective-permute-start.66 = (bf16[2,64,1,1024]{3,1,0,2:T(8,128)(2,1)}, bf16[2,64,1,1024]{3,1,0,2:T(8,128)(2,1)}, u32[]{:S(2)}, u32[]{:S(2)}) collective-permute-start(bf16[2,64,1,1024]{3,1,0,2:T(8,128)(2,1)} %get-tuple-element.53), channel_id=1, source_target_pairs={{0,8},{1,9},{2,10},{3,11},{4,12},{5,13},{6,14},{7,15},{8,16},{9,17... | collective-permute-start | bytes 786440 | tf_op jit(solution)/shard_map/ppermute | solution.py:50
  671.3 120.6 %collective-permute-start.71 = (bf16[1,256,2048]{2,1,0:T(8,128)(2,1)S(1)}, bf16[1,256,2048]{2,1,0:T(8,128)(2,1)S(1)}, u32[]{:S(2)}, u32[]{:S(2)}) collective-permute-start(bf16[1,256,2048]{2,1,0:T(8,128)(2,1)S(1)} %fusion.37), channel_id=1, source_target_pairs={{0,2},{1,3},{2,0},{3,1},{4,6},{5,7},{6,4},{7,5},{8,10},{9,11},{10,... | collective-permute-start | bytes 3145736 | tf_op jit(solution)/shard_map/ppermute | solution.py:50
  (98 other events, 1653.7 us)
Sparse Core Ops, SparseCore 0:
  649.7 121.1 all-reduce.3
